TPU v7x, 128 devices: a whole 4x4x4 slice. The times are simulated.
128 devices in a mesh: dp: 8 (over z_hi, x), tensor: 16 (over y, z_lo, core).
Axes of the slice: x: 4, y: 4, z: 4 (z_hi: 2, z_lo: 2; z = z_hi * 2 + z_lo), core: 2. Of those that a mesh axis runs over, the one named last changes fastest.
Arguments:
- picture_embeds: bfloat16 [1024, 6144], P(('dp', 'tensor')), may hold values from -6 to 6
- caption_embeds: bfloat16 [1024, 6144], P(('dp', 'tensor')), may hold values from -6 to 6
- picture_match_ids: int32 [1024], replicated, may hold values from 0 to 511
- caption_match_ids: int32 [1024], replicated, may hold values from 0 to 511
- logit_multiplier: float32 [1], replicated, may hold values from 10 to 40
- logit_offset: float32 [1], replicated, may hold values from -4 to -1
- branch_entries: bfloat16 [16384, 6144], P(('dp', 'tensor')), may hold values from -64 to 64, as said below
- rescale_factor: float32 [6144], replicated, may hold values from 0.1 to 1.9
- entry_projection_matrix: bfloat16 [6144, 12288], P(None, 'tensor'), may hold values from -0.078125 to 0.078125
- exit_projection_matrix: bfloat16 [12288, 6144], P('tensor'), may hold values from -0.0546875 to 0.0546875
Outputs:
- image_grad: float32 [1024, 6144], P(('dp', 'tensor'))
- token_grad: float32 [16384, 6144], P(('dp', 'tensor'))
Inputs may be any that keep to these rules, and one draw needn't show every extreme that they name: `branch_entries`: token rows.
All inputs are finite; a program needn't handle non-finite values.
Results may differ from a plain program's by a relative error of at most 0.0047.
Values may be sent and summed in bfloat16 or wider, within the bound.
A program may use at most 192 MiB of HBM per device.

v0:
```python
import jax
import jax.numpy as jnp
from jax import lax
from jax.sharding import PartitionSpec as P

PATCHES = 256


epsilon = 1e-06


def unit_rows(rows):
    values = rows.astype(jnp.float32)
    scale = lax.rsqrt(jnp.sum(values * values, axis=-1) + epsilon)
    return (scale, values * scale[:, None])


def layer_stats(rows):
    values = rows.astype(jnp.float32)
    centered = values - jnp.mean(values, axis=-1, keepdims=True)
    inverse = lax.rsqrt(jnp.mean(centered * centered, axis=-1, keepdims=True) + epsilon)
    return (inverse, centered * inverse)


def gelu_slope(values):
    cumulative = 0.5 * (1.0 + lax.erf(values * 0.7071067811865476))
    density = jnp.exp(-0.5 * values * values) * 0.3989422804014327
    return cumulative + values * density


def unit_backward(scale, unit, grad):
    return scale[:, None] * (grad - unit * jnp.sum(unit * grad, axis=-1, keepdims=True))


def trailing_axis_dot(left, right):
    return lax.dot_general(
        left, right, (((1,), (1,)), ((), ())), preferred_element_type=jnp.float32
    )


def body(
    picture_embeds,
    caption_embeds,
    picture_match_ids,
    caption_match_ids,
    logit_multiplier,
    logit_offset,
    branch_entries,
    rescale_factor,
    entry_projection_matrix,
    exit_projection_matrix,
):
    tensor_size = lax.axis_size("tensor")
    tensor_rank = lax.axis_index("tensor")
    batch_rank = lax.axis_index("dp")
    emb_rows = picture_embeds.shape[0]
    group_img = emb_rows * tensor_size
    tok_rows = branch_entries.shape[0]
    group_tok = tok_rows * tensor_size
    micro_img = group_tok // PATCHES
    multiplier_scalar = logit_multiplier[0]
    offset_scalar = logit_offset[0]
    own_inverse, own_normed = layer_stats(branch_entries)
    group_emb, group_tokens = (
        lax.all_gather(picture_embeds, "tensor", axis=0, tiled=True),
        lax.all_gather(branch_entries, "tensor", axis=0, tiled=True),
    )
    _, group_normed = layer_stats(group_tokens)
    ln_input = (group_normed * rescale_factor).astype(jnp.bfloat16)
    img_scale, img_exact = unit_rows(group_emb)
    picture_direction = img_exact.astype(jnp.bfloat16)
    img_ids = lax.dynamic_slice_in_dim(picture_match_ids, batch_rank * group_img, group_img)
    cycle_ids = lax.dynamic_index_in_dim(
        caption_match_ids.reshape(-1, tensor_size, emb_rows), tensor_rank, 1, keepdims=False
    ).reshape(-1)
    _, piece_exact = unit_rows(lax.all_gather(caption_embeds, "dp", axis=0, tiled=True))
    fragment_direction = piece_exact.astype(jnp.bfloat16)
    similarity_scores = (
        multiplier_scalar * trailing_axis_dot(picture_direction, fragment_direction) + offset_scalar
    )
    match_signs = jnp.where(img_ids[:, None] == cycle_ids[None, :], 1.0, -1.0).astype(jnp.float32)
    loss_multiplier = (
        -match_signs * multiplier_scalar * jax.nn.sigmoid(-match_signs * similarity_scores)
    ).astype(jnp.bfloat16)
    loss_multiplier, fragment_direction = (loss_multiplier, fragment_direction)
    folded = jnp.dot(loss_multiplier, fragment_direction, preferred_element_type=jnp.float32)

    def unit_terms(count):
        return lax.slice_in_dim(folded, 0, count, axis=0)

    own_sums = lax.psum_scatter(
        unit_terms(lax.axis_size("tensor") * emb_rows), "tensor", scatter_dimension=0, tiled=True
    )
    micro_sums = lax.psum(unit_terms(micro_img), "tensor")
    own_scale, own_exact = unit_rows(picture_embeds)
    image_grad = unit_backward(own_scale, own_exact, own_sums)
    micro_grad = unit_backward(img_scale[:micro_img], img_exact[:micro_img], micro_sums)
    hidden_units = entry_projection_matrix.shape[1]
    pre_act = jnp.dot(ln_input, entry_projection_matrix, preferred_element_type=jnp.float32)
    hidden_grad = trailing_axis_dot(micro_grad.astype(jnp.bfloat16), exit_projection_matrix)
    slope = gelu_slope(pre_act.reshape(micro_img, PATCHES, hidden_units))
    pre_grad = (
        (hidden_grad[:, None, :] * slope).reshape(group_tok, hidden_units).astype(jnp.bfloat16)
    )
    ln_grad = lax.psum_scatter(
        trailing_axis_dot(pre_grad, entry_projection_matrix),
        "tensor",
        scatter_dimension=0,
        tiled=True,
    )
    own_image = tensor_rank * tok_rows // PATCHES
    own_cot = lax.dynamic_index_in_dim(micro_grad, own_image, 0, keepdims=True)
    scaled = ln_grad * rescale_factor
    token_grad = own_cot + own_inverse * (
        scaled
        - jnp.mean(scaled, axis=-1, keepdims=True)
        - own_normed * jnp.mean(scaled * own_normed, axis=-1, keepdims=True)
    )
    return (image_grad, token_grad)


def solution(mesh):
    in_specs = (
        P(("dp", "tensor"), None),
        P(("dp", "tensor"), None),
        P(),
        P(),
        P(),
        P(),
        P(("dp", "tensor"), None),
        P(),
        P(None, "tensor"),
        P("tensor", None),
    )
    out_specs = (P(("dp", "tensor"), None), P(("dp", "tensor"), None))
    return jax.shard_map(body, mesh=mesh, in_specs=in_specs, out_specs=out_specs, check_vma=False)
```

profile of v0, /device:TPU:1, one launch (start us, length us, event | category | flops | bytes accessed | tf_op | source)
XLA Modules:
  0.0 913.2 jit_solution(15427386735743517159)
XLA Ops:
  7.2 0.0 all-gather.3.cloned.1.call-start
  7.2 0.7 all-gather.3.cloned.1.call-update
  7.9 0.0 all-reduce.2.cloned.1.call-start
  9.2 0.8 reshape.62
  10.0 0.1 eq.16
  10.1 0.8 dynamic_slice.11
  10.9 32.7 %all_gather.10 = bf16[64,6144]{1,0:T(8,128)(2,1)S(1)} all-gather(bf16[8,6144]{1,0:T(8,128)(2,1)} %param.11), channel_id=1, replica_groups=mesh['dp'=8,'tensor'=16] {'dp'}, dimensions={0}, use_global_device_ids=true | all-gather | bytes 884736 | tf_op jit(solution)/shard_map/all_gather | solution.py:76
  43.6 0.3 fusion.28
  43.8 3.3 all-gather.3.cloned.1.call-done
  47.1 1.8 fusion.27
  48.9 5.0 fusion.60
  54.0 0.0 copy-start.2
  54.0 1.7 slice.12
  55.7 0.0 all-reduce.2.cloned.1.call-update
  55.7 0.0 all-gather.5.cloned.1.call-start
  55.8 0.7 all-gather.5.cloned.1.call-update
  56.5 0.0 reduce-scatter.3.cloned.1.call-start
  56.5 0.5 reduce-scatter.3.cloned.1.call-update
  57.0 0.2 reduce-scatter.5.cloned.1.call-start
  57.3 0.0 copy-done.2
  57.3 2.1 convert_multiply_fusion
  59.4 109.4 %all-reduce.2.cloned.1.call-done = f32[8,6144]{1,0:T(8,128)} async-done(((f32[8,6144]{1,0:T(8,128)}), f32[8,6144]{1,0:T(8,128)}) %all-reduce.2.cloned.1.call-update) | async-done | bytes 196624 | tf_op jit(solution)/shard_map/psum | solution.py:94
  168.9 1.2 multiply_reduce_fusion.1
  170.0 1.1 subtract_multiply_fusion
  171.2 6.2 fusion.72
  177.4 124.7 %all-gather.5.cloned.1.call-done = bf16[2048,6144]{1,0:T(8,128)(2,1)} async-done(((bf16[128,6144]{1,0:T(8,128)(2,1)}), bf16[2048,6144]{1,0:T(8,128)(2,1)}) %all-gather.5.cloned.1.call-update) | async-done | bytes 25165840 | tf_op jit(solution)/shard_map/all_gather | solution.py:66
  302.0 12.0 %convert_reduce_fusion = f32[2048]{0:T(1024)S(1)} fusion(bf16[2048,6144]{1,0:T(8,128)(2,1)} %all-gather.5.cloned.1.call-done), kind=kLoop, calls=%fused_computation.1 | loop fusion | flops 25163776 | bytes 25174016 | tf_op jit(solution)/shard_map/reduce_sum | solution.py:20
  314.0 3.7 copy-done
  317.7 9.9 %fusion.2 = f32[2048]{0:T(1024)S(1)} fusion(bf16[2048,6144]{1,0:T(8,128)(2,1)S(1)} %copy-done, f32[2048]{0:T(1024)S(1)} %broadcast_multiply_fusion), kind=kLoop, calls=%fused_computation.4 | loop fusion | flops 50329600 | bytes 25182208 | tf_op jit(solution)/shard_map/reduce_sum | solution.py:21
  327.6 0.0 slice-done
  327.6 0.0 slice-done.1
  327.6 0.0 copy-done.5
  327.6 0.0 slice-done.2
  327.7 26.0 %fusion.15 = bf16[2048,768]{1,0:T(8,128)(2,1)S(1)} fusion(bf16[6144,768]{1,0:T(8,128)(2,1)S(1)} %bitcast.15, bf16[2048,6144]{1,0:T(8,128)(2,1)} %all-gather.5.cloned.1.call-done, f32[6144]{0:T(1024)S(1)} %copy-done.5, f32[2048]{0:T(1024)S(1)} %add_rsqrt_fusion, f32[2048]{0:T(1024)S(1)} %broadcast_multiply_fusion, f32[8,768]{1,0:T(8,128)S(1)} %fusion.72), kind=kOutput, calls=%fused_computation.17 | convolution fusion | flops 19405996032 | bytes 37814272 | tf_op jit(solution)/shard_map/dot_general | solution.py:99
  353.6 28.5 %fusion.86 = f32[2048,6144]{1,0:T(8,128)} fusion(bf16[2048,768]{1,0:T(8,128)(2,1)S(1)} %fusion.15, bf16[6144,768]{1,0:T(8,128)(2,1)} %param.18), kind=kOutput, calls=%fused_computation.85 | convolution fusion | flops 19327352832 | bytes 62914560 | tf_op jit(solution)/shard_map/dot_general | solution.py:36
  382.1 0.0 reduce-scatter.5.cloned.1.call-update
  382.2 0.8 copy-done.4
  383.0 0.2 fusion.71
  383.2 0.4 copy-done.1
  383.6 0.3 convert_reduce_fusion.1
  383.9 0.6 fusion.26
  384.5 0.0 reduce-scatter.3.cloned.1.call-done
  384.6 1.2 fusion.68
  385.7 1.7 fusion.70
  387.4 513.5 %reduce-scatter.5.cloned.1.call-done = f32[128,6144]{1,0:T(8,128)} async-done(((f32[2048,6144]{1,0:T(8,128)}), f32[128,6144]{1,0:T(8,128)}) %reduce-scatter.5.cloned.1.call-update) | async-done | bytes 3145744 | tf_op jit(solution)/shard_map/reduce_scatter | solution.py:105
  900.9 3.0 multiply_reduce_fusion
  903.9 0.0 copy-done.3
  903.9 2.8 fusion.25
  (19 shorter events, 0.1 us)
Async XLA Ops:
  7.2 40.0 %all-gather.3.cloned.1.call-start = ((), (), s32[]{:S(2)}) async-start(), calls=%async_computation.2 | async-start | bytes 1671168 | tf_op jit(solution)/shard_map/all_gather | solution.py:65
  7.9 161.0 %all-reduce.2.cloned.1.call-start = ((), (), s32[]{:S(2)}) async-start(), calls=%async_computation.4 | async-start | bytes 393216 | tf_op jit(solution)/shard_map/psum | solution.py:94
  54.0 3.3 copy-start.2
  55.7 246.3 %all-gather.5.cloned.1.call-start = ((), (), s32[]{:S(2)}) async-start(), calls=%async_computation.5 | async-start | bytes 26738688 | tf_op jit(solution)/shard_map/all_gather | solution.py:66
  56.5 328.1 %reduce-scatter.3.cloned.1.call-start = ((), (), s32[]{:S(2)}) async-start(), calls=%async_computation.3 | async-start | bytes 3342336 | tf_op jit(solution)/shard_map/reduce_scatter | solution.py:91
  57.0 843.8 %reduce-scatter.5.cloned.1.call-start = ((), (), s32[]{:S(2)}) async-start(), calls=%async_computation.6 | async-start | bytes 53477376 | tf_op jit(solution)/shard_map/reduce_scatter | solution.py:105
  302.0 15.7 %copy-start = (bf16[2048,6144]{1,0:T(8,128)(2,1)S(1)}, bf16[2048,6144]{1,0:T(8,128)(2,1)}, u32[]{:S(2)}) copy-start(bf16[2048,6144]{1,0:T(8,128)(2,1)} %all-gather.5.cloned.1.call-done) | copy-start | bytes 75497472
  302.0 25.6 %slice-start = ((s8[9437184]{0:T(1024)(128)(4,1)}), s8[4194304]{0:T(1024)(128)(4,1)S(1)}, s32[]{:S(2)}) async-start(s8[9437184]{0:T(1024)(128)(4,1)} %bitcast.14), calls=%async_computation.7 | async-start | bytes 8388608
  302.0 25.6 %slice-start.1 = ((s8[9437184]{0:T(1024)(128)(4,1)}), s8[4194304]{0:T(1024)(128)(4,1)S(1)}, s32[]{:S(2)}) async-start(s8[9437184]{0:T(1024)(128)(4,1)} %bitcast.14), calls=%async_computation.8 | async-start | bytes 8388608
  317.7 9.9 %copy-start.5 = (f32[6144]{0:T(1024)S(1)}, f32[6144]{0:T(1024)}, u32[]{:S(2)}) copy-start(f32[6144]{0:T(1024)} %param.17) | copy-start | bytes 73732
  317.7 9.9 %slice-start.2 = ((s8[9437184]{0:T(1024)(128)(4,1)}), s8[1048576]{0:T(1024)(128)(4,1)S(1)}, s32[]{:S(2)}) async-start(s8[9437184]{0:T(1024)(128)(4,1)} %bitcast.14), calls=%async_computation.9 | async-start | bytes 2097152
  382.1 0.9 copy-start.4
  382.1 1.5 copy-start.1
  900.9 3.0 copy-start.3
Sparse Core Ops, SparseCore 0:
  9.7 37.3 all-gather.2
  55.8 112.9 all-reduce.1
  170.7 131.3 all-gather.4
  305.0 62.5 reduce-scatter.2
  382.3 518.5 reduce-scatter.4
where the time goes:
time: 914 us; the launch traced here: 913 us
  waiting for transfers between devices  753 us (82%)
  matrix products  65.7 us (7%)
  other arithmetic  38 us (4%)
  blocking collectives  32.7 us (4%)
  between operations  15.3 us (2%)
    reduce_scatter x1, waiting for transfers between devices, body(): lax.psum_scatter(trailing_axis_dot(pre_grad, entry_projection_matrix), 't...  513 us
    all_gather x1, waiting for transfers between devices, body(): lax.all_gather(branch_entries, 'tensor', axis=0, tiled=True)  125 us
    psum x1, waiting for transfers between devices, body(): micro_sums = lax.psum(unit_terms(micro_img), 'tensor')  109 us
    dot_general x2, matrix products, trailing_axis_dot(): lax.dot_general(left, right, (((1,), (1,)), ((), ())), preferred_element_...  34.7 us
    all_gather x1, blocking collectives, body(): lax.all_gather(caption_embeds, 'dp', axis=0, tiled=True)  32.7 us
    dot_general x1, matrix products, body(): jnp.dot(ln_input, entry_projection_matrix, preferred_element_type=jnp.flo...  26 us
  transfers between devices with their start and end apart: 5, of which 4 were waited for; matrix products, arithmetic and copies ran while one was open for 10% of the time, Pallas kernels for 0%

commit v1 on v0

v1 whole, which is shorter than its diff:
```python
import jax
import jax.numpy as jnp
from jax import lax
from jax.experimental import pallas as pl
from jax.experimental.pallas import tpu as pltpu
from jax.sharding import PartitionSpec as P

EPS = 1e-06
MESH = pl.DeviceIdType.MESH
F32 = jnp.float32
BF16 = jnp.bfloat16
D = 6144
HALF = D // 2
HB = 768
ROWS = 128
CH = 512
N = D // CH
AHEAD = 3


def gelu_slope(values):
    cumulative = 0.5 * (1.0 + lax.erf(values * 0.7071067811865476))
    density = jnp.exp(-0.5 * values * values) * 0.3989422804014327
    return cumulative + values * density


def dot_nt(left, right):
    return lax.dot_general(left, right, (((1,), (1,)), ((), ())), preferred_element_type=F32)


def kernel(
    pic_ref, cap_ref, img_ids, txt_ids, mult_ref, offs_ref, tok_ref, gain_ref, w1, wx_hbm,
    img_out, tok_out, w3,
    ln, wbuf, pre, grad, m1o, m2o, m1i, m2i, text, wx, stack, unit, fold, fold_in, tx, exact, cot, cotf, hid, stat,
    s_send, s_tok, s_fwd, s_z, s_x, s_own, s_for, s_m1, s_m2, s_small, s_hid, s_w, s_wx,
):
    d = lax.axis_index("dp")
    t = lax.axis_index("tensor")
    x, zh = d % 4, d // 4
    y, zl, c = t // 4, (t // 2) % 2, t % 2
    z = 2 * zh + zl

    def dev(x_, y_, z_, c_):
        return ((z_ // 2) * 4 + x_, y_ * 4 + (z_ % 2) * 2 + c_)

    yp, ym = dev(x, (y + 1) % 4, z, c), dev(x, (y + 3) % 4, z, c)
    zp, zm = dev(x, y, (z + 1) % 4, c), dev(x, y, (z + 3) % 4, c)
    xp, xm = dev((x + 1) % 4, y, z, c), dev((x + 3) % 4, y, z, c)
    mate = (d, y * 4 + zl * 2 + (1 - c))

    def send(src, dst, ssem, rsem, device):
        pltpu.make_async_remote_copy(
            src_ref=src, dst_ref=dst, send_sem=ssem, recv_sem=rsem, device_id=device, device_id_type=MESH
        ).start()

    def wait(ref, sem):
        pltpu.make_async_copy(ref, ref, sem).wait()

    slot = d * 2 + zl

    def text_peer(s):
        other = (slot + s) % 16
        return (other // 2, y * 4 + (other % 2) * 2 + c)

    bar = pltpu.get_barrier_semaphore()

    def greet(s, _):
        pl.semaphore_signal(bar, 1, device_id=text_peer(s), device_id_type=MESH)
        pl.semaphore_signal(bar, 1, device_id=(d, (t + s) % 16), device_id_type=MESH)
        return 0

    lax.fori_loop(1, 16, greet, 0)

    pltpu.make_async_copy(wx_hbm, wx, s_wx).start()

    img = pic_ref[...].astype(F32)
    img_scale = lax.rsqrt(jnp.sum(img * img, axis=-1, keepdims=True) + EPS)
    img_exact = img * img_scale
    exact[...] = img_exact
    stat[2, 0:8] = jnp.broadcast_to(img_scale, (8, 128))
    stack[y] = jnp.concatenate([img_exact[:, :HALF], img_exact[:, HALF:]], axis=0).astype(BF16)
    cap = cap_ref[...].astype(F32)
    tx[c] = cap * lax.rsqrt(jnp.sum(cap * cap, axis=-1, keepdims=True) + EPS)

    def norm_rows(i, _):
        rows = pl.ds(pl.multiple_of(i * 16, 16), 16)
        values = tok_ref[rows, :].astype(F32)
        mean = jnp.mean(values, axis=-1, keepdims=True)
        centered = values - mean
        inverse = lax.rsqrt(jnp.mean(centered * centered, axis=-1, keepdims=True) + EPS)
        stat[0, rows] = jnp.broadcast_to(mean, (16, 128))
        stat[1, rows] = jnp.broadcast_to(inverse, (16, 128))
        out = (centered * inverse * gain_ref[...]).astype(BF16)
        for k in range(N):
            ln[k, rows, :] = out[:, k * CH:(k + 1) * CH]
        return 0

    lax.fori_loop(0, ROWS // 16, norm_rows, 0)

    pl.semaphore_wait(bar, 30)

    send(tx.at[c], tx.at[c], s_small.at[0], s_small.at[1], mate)

    def send_images(r, _):
        send(stack.at[y], stack.at[y], s_small.at[2], s_small.at[3], dev(x, (y + r) % 4, z, c))
        return 0

    lax.fori_loop(1, 4, send_images, 0)

    xpar = x % 2

    def piece(k, par, p):
        return pl.ds(pl.multiple_of(k * CH + par * 256 + p * 128, 128), 128)

    def chunk(k):
        return pl.ds(pl.multiple_of(k * CH, CH), CH)

    def send_own(k):
        send(ln.at[k, pl.ds(0, 128)], ln.at[k, pl.ds(384, 128)], s_send.at[0], s_tok.at[0, k], yp)
        send(ln.at[k, pl.ds(0, 128)], ln.at[k, pl.ds(128, 128)], s_send.at[1], s_tok.at[1, k], ym)
        send(w1.at[piece(k, xpar, 0)], w3.at[1, piece(k, xpar, 0)], s_send.at[2], s_z.at[0, k], zm)
        send(w1.at[piece(k, xpar, 1)], w3.at[1, piece(k, xpar, 1)], s_send.at[3], s_z.at[1, k], zp)
        send(w1.at[chunk(k)], w3.at[0, chunk(k)], s_send.at[4], s_own.at[k], mate)

    def first(k, _):
        send_own(k)
        return 0

    lax.fori_loop(0, AHEAD, first, 0)

    wait(tx.at[0], s_small.at[1])
    both = jnp.concatenate([tx[0], tx[1]], axis=0)
    mine = jnp.where(c == 0, both[:, :HALF], both[:, HALF:]).astype(BF16)
    text_rows = pl.ds(pl.multiple_of(slot * 16, 16), 16)
    text_cols = pl.ds(pl.multiple_of(c * HALF, HALF), HALF)
    text[text_rows, text_cols] = mine

    def send_texts(s, _):
        part = text.at[text_rows, text_cols]
        send(part, part, s_small.at[4], s_small.at[5], text_peer(s))
        return 0

    lax.fori_loop(1, 16, send_texts, 0)
    pre[...] = jnp.zeros_like(pre)

    def load(k, b):
        pltpu.make_async_copy(w1.at[chunk(k)], wbuf.at[b, :, pl.ds(0, HB)], s_w.at[b]).start()
        for j in range(3):
            pltpu.make_async_copy(w3.at[j, chunk(k)], wbuf.at[b, :, pl.ds((j + 1) * HB, HB)], s_w.at[b]).start()

    def gather_step(k, _):
        @pl.when(k < N)
        def _():
            wait(ln.at[0, pl.ds(0, 128)], s_tok.at[0, k])
            wait(ln.at[0, pl.ds(0, 128)], s_tok.at[1, k])
            send(ln.at[k, pl.ds(384, 64)], ln.at[k, pl.ds(256, 64)], s_send.at[5], s_fwd.at[0, k], yp)
            send(ln.at[k, pl.ds(192, 64)], ln.at[k, pl.ds(320, 64)], s_send.at[6], s_fwd.at[1, k], ym)
            wait(w3.at[1, pl.ds(0, 128)], s_z.at[0, k])
            wait(w3.at[1, pl.ds(0, 128)], s_z.at[1, k])
            send(w3.at[1, piece(k, xpar, 0)], w3.at[1, piece(k, xpar, 0)], s_send.at[7], s_x.at[0, k], xm)
            send(w3.at[1, piece(k, xpar, 1)], w3.at[1, piece(k, xpar, 1)], s_send.at[8], s_x.at[1, k], xp)

        @pl.when(k + AHEAD < N)
        def _():
            send_own(k + AHEAD)

        @pl.when(jnp.logical_and(k >= 1, k < N + 1))
        def _():
            q = k - 1
            wait(ln.at[0, pl.ds(0, 64)], s_fwd.at[0, q])
            wait(ln.at[0, pl.ds(0, 64)], s_fwd.at[1, q])
            wait(w3.at[1, pl.ds(0, 128)], s_x.at[0, q])
            wait(w3.at[1, pl.ds(0, 128)], s_x.at[1, q])
            send(w3.at[1, chunk(q)], w3.at[2, chunk(q)], s_send.at[9], s_for.at[q], mate)

        @pl.when(jnp.logical_and(k >= 2, k < N + 2))
        def _():
            q = k - 2
            wait(w3.at[0, pl.ds(0, CH)], s_own.at[q])
            wait(w3.at[2, pl.ds(0, CH)], s_for.at[q])
            load(q, q % 2)

        @pl.when(k >= 3)
        def _():
            q = k - 3
            b = q % 2
            wait(wbuf.at[b], s_w.at[b])

            def columns(j, _):
                cols = pl.ds(pl.multiple_of(j * HB, HB), HB)
                pre[:, cols] += jnp.dot(ln[q], wbuf[b, :, cols], preferred_element_type=F32)
                return 0

            lax.fori_loop(0, 4, columns, 0)

        @pl.when(k == 1)
        def _():
            wait(text.at[pl.ds(0, 240), pl.ds(0, HALF)], s_small.at[5])
            half = text.at[:, text_cols]
            send(half, half, s_small.at[6], s_small.at[7], mate)

        @pl.when(k == 2)
        def _():
            wait(stack.at[pl.ds(0, 3)], s_small.at[3])
            wait(text.at[:, pl.ds(0, HALF)], s_small.at[7])
            for pair in range(2):
                a = stack[2 * pair].astype(F32)
                b = stack[2 * pair + 1].astype(F32)
                unit[pair * 16:(pair + 1) * 16, :HALF] = jnp.concatenate([a[:8], b[:8]], axis=0).astype(BF16)
                unit[pair * 16:(pair + 1) * 16, HALF:] = jnp.concatenate([a[8:], b[8:]], axis=0).astype(BF16)
            multiplier = mult_ref[0]
            logits = multiplier * dot_nt(unit[...], text[...]) + offs_ref[0]
            labels = jnp.where(img_ids[...] == txt_ids[...], 1.0, -1.0).astype(F32)
            coef = (-labels * multiplier * jax.nn.sigmoid(-labels * logits)).astype(BF16)

            def fold_cols(j, _):
                cols = pl.ds(pl.multiple_of(j * 1024, 1024), 1024)
                part = jnp.dot(coef, text[:, cols], preferred_element_type=F32)
                for i in range(4):
                    fold[i, :, cols] = part[i * 8:(i + 1) * 8]
                return 0

            lax.fori_loop(0, 6, fold_cols, 0)

            def send_sums(r, _):
                other = (y + r) % 4
                send(fold.at[other], fold_in.at[r - 1], s_small.at[8], s_small.at[9], dev(x, other, z, c))
                return 0

            lax.fori_loop(1, 4, send_sums, 0)

        @pl.when(k == 4)
        def _():
            wait(fold_in, s_small.at[9])
            total = fold[y] + fold_in[0] + fold_in[1] + fold_in[2]
            ex = exact[...]
            scale = stat[2, 0:8, 0:1]
            g = scale * (total - ex * jnp.sum(ex * total, axis=-1, keepdims=True))
            img_out[...] = g

            @pl.when(t == 0)
            def _():
                cot[...] = jnp.concatenate([g[:, :HALF], g[:, HALF:]], axis=0).astype(BF16)

                def send_cot(s, _):
                    send(cot, cot, s_small.at[10], s_small.at[11], (d, s))
                    return 0

                lax.fori_loop(1, 16, send_cot, 0)

        @pl.when(k == 6)
        def _():
            @pl.when(t != 0)
            def _():
                wait(cot, s_small.at[11])

            cotf[...] = cot[...].astype(F32)
            wait(wx, s_wx)
            for j in range(3):
                low = dot_nt(cot[...], wx[j * 256:(j + 1) * 256, :HALF])
                high = dot_nt(cot[...], wx[j * 256:(j + 1) * 256, HALF:])
                hid[0, :, j * 256:(j + 1) * 256] = low[:8] + high[8:]
            send(hid.at[0], hid.at[1], s_small.at[12], s_hid.at[0], mate)
            send(hid.at[0], hid.at[2], s_small.at[13], s_hid.at[1], (d, y * 4 + (1 - zl) * 2 + c))
            send(hid.at[0], hid.at[3], s_small.at[14], s_hid.at[2], (d, y * 4 + (1 - zl) * 2 + (1 - c)))

        return 0

    lax.fori_loop(0, N + 3, gather_step, 0)
    load(0, 0)
    for j in range(3):
        wait(hid.at[0], s_hid.at[j])

    def slope_block(i, _):
        r, j = i // 4, i % 4
        rows = pl.ds(pl.multiple_of(r * ROWS, ROWS), ROWS)
        cols = pl.ds(pl.multiple_of(j * HB, HB), HB)
        image = ((y + r) % 4) * 2 + zl
        factor = hid[j, pl.ds(image, 1), :]
        grad[rows, cols] = (factor * gelu_slope(pre[rows, cols])).astype(BF16)
        return 0

    lax.fori_loop(0, 16, slope_block, 0)

    def pend(n, side):
        return (
            pl.ds(pl.multiple_of((n // 6) * 128 + side * 64, 64), 64),
            pl.ds(pl.multiple_of((n % 6) * CH, CH), CH),
        )

    def kept(n):
        return (
            pl.ds(pl.multiple_of(256 + (n // 6) * 128, 128), 128),
            pl.ds(pl.multiple_of((n % 6) * CH, CH), CH),
        )

    def scatter_step(n, carry):
        @pl.when(n + 1 < N)
        def _():
            load(n + 1, (n + 1) % 2)

        @pl.when(n < N)
        def _():
            b = n % 2
            wait(wbuf.at[b], s_w.at[b])
            part = dot_nt(grad[...], wbuf[b])
            m1o[n, 0] = part[256:320].astype(BF16)
            m1o[n, 1] = part[320:384].astype(BF16)
            send(m1o.at[n, 0], m1i.at[n, 0], s_send.at[10], s_m1.at[0, n], yp)
            send(m1o.at[n, 1], m1i.at[n, 1], s_send.at[11], s_m1.at[1, n], ym)
            pre[pend(n, 0)] = part[128:192]
            m2o[n, 0, 64:128] = part[192:256].astype(BF16)
            m2o[n, 1, 0:64] = part[384:448].astype(BF16)
            pre[pend(n, 1)] = part[448:512]
            pre[kept(n)] = part[0:128]

        @pl.when(jnp.logical_and(n >= 2, n < N + 2))
        def _():
            q = n - 2
            wait(m1i.at[0, 0], s_m1.at[0, q])
            m2o[q, 0, 0:64] = (pre[pend(q, 0)] + m1i[q, 0].astype(F32)).astype(BF16)
            send(m2o.at[q, 0], m2i.at[q, 0], s_send.at[12], s_m2.at[0, q], yp)
            wait(m1i.at[0, 0], s_m1.at[1, q])
            m2o[q, 1, 64:128] = (pre[pend(q, 1)] + m1i[q, 1].astype(F32)).astype(BF16)
            send(m2o.at[q, 1], m2i.at[q, 1], s_send.at[13], s_m2.at[1, q], ym)

        @pl.when(n >= 5)
        def _():
            q = n - 5
            wait(m2i.at[0, 0], s_m2.at[0, q])
            wait(m2i.at[0, 0], s_m2.at[1, q])
            cols = chunk(q)
            total = pre[kept(q)] + m2i[q, 0].astype(F32) + m2i[q, 1].astype(F32)
            e = total * gain_ref[:, cols]
            normed = (tok_ref[:, cols].astype(F32) - stat[0, :, 0:1]) * stat[1, :, 0:1]
            pre[kept(q)] = e
            stat[3] += jnp.broadcast_to(jnp.sum(e, axis=-1, keepdims=True), (128, 128))
            stat[4] += jnp.broadcast_to(jnp.sum(e * normed, axis=-1, keepdims=True), (128, 128))

        return carry

    stat[3] = jnp.zeros((128, 128), F32)
    stat[4] = jnp.zeros((128, 128), F32)
    lax.fori_loop(0, N + 5, scatter_step, 0)

    own_image = t // 2

    def finish(q, _):
        cols = chunk(q)
        inverse = stat[1, :, 0:1]
        normed = (tok_ref[:, cols].astype(F32) - stat[0, :, 0:1]) * inverse
        cot_cols = pl.ds(pl.multiple_of((q % 6) * CH, CH), CH)
        row = cotf[pl.ds((q // 6) * 8 + own_image, 1), cot_cols]
        tok_out[:, cols] = row + inverse * (
            pre[kept(q)] - stat[3, :, 0:1] * (1.0 / D) - normed * (stat[4, :, 0:1] * (1.0 / D))
        )
        return 0

    lax.fori_loop(0, N, finish, 0)

    wait(tx.at[0], s_small.at[0])
    wait(stack.at[pl.ds(0, 3)], s_small.at[2])
    wait(text.at[pl.ds(0, 240), pl.ds(0, HALF)], s_small.at[4])
    wait(text.at[:, pl.ds(0, HALF)], s_small.at[6])
    wait(fold_in, s_small.at[8])

    @pl.when(t == 0)
    def _():
        for _i in range(15):
            wait(cot, s_small.at[10])

    for j in range(3):
        wait(hid.at[0], s_small.at[12 + j])
    for j in range(2):
        wait(ln.at[:, pl.ds(0, 128)], s_send.at[j])
        wait(w1.at[pl.ds(0, N * 128)], s_send.at[2 + j])
        wait(ln.at[:, pl.ds(0, 64)], s_send.at[5 + j])
        wait(w1.at[pl.ds(0, N * 128)], s_send.at[7 + j])
        wait(m1o.at[:, 0], s_send.at[10 + j])
        wait(m2o.at[:, 0], s_send.at[12 + j])
    wait(w1, s_send.at[4])
    wait(w1, s_send.at[9])


def body(
    picture_embeds, caption_embeds, picture_match_ids, caption_match_ids, logit_multiplier, logit_offset,
    branch_entries, rescale_factor, entry_projection_matrix, exit_projection_matrix,
):
    d = lax.axis_index("dp")
    t = lax.axis_index("tensor")
    img_ids = picture_match_ids.reshape(8, 4, 4, 8)
    img_ids = lax.dynamic_slice(img_ids, (d, 0, t % 4, 0), (1, 4, 1, 8)).reshape(32, 1)
    txt_ids = caption_match_ids.reshape(8, 4, 4, 8)
    txt_ids = lax.dynamic_slice(txt_ids, (0, t // 4, 0, 0), (8, 1, 4, 8)).reshape(1, 256)
    vmem = pl.BlockSpec(memory_space=pltpu.VMEM)
    smem = pl.BlockSpec(memory_space=pltpu.SMEM)
    anyw = pl.BlockSpec(memory_space=pl.ANY)
    dma = pltpu.SemaphoreType.DMA
    image_grad, token_grad, _ = pl.pallas_call(
        kernel,
        out_shape=(
            jax.ShapeDtypeStruct((8, D), F32),
            jax.ShapeDtypeStruct((ROWS, D), F32),
            jax.ShapeDtypeStruct((3, D, HB), BF16),
        ),
        in_specs=[vmem, vmem, vmem, vmem, smem, smem, vmem, vmem, anyw, anyw],
        out_specs=(vmem, vmem, anyw),
        scratch_shapes=[
            pltpu.VMEM((N, 4 * ROWS, CH), BF16),
            pltpu.VMEM((2, CH, 4 * HB), BF16),
            pltpu.VMEM((4 * ROWS, 4 * HB), F32),
            pltpu.VMEM((4 * ROWS, 4 * HB), BF16),
            pltpu.VMEM((N, 2, 64, CH), BF16),
            pltpu.VMEM((N, 2, 128, CH), BF16),
            pltpu.VMEM((N, 2, 64, CH), BF16),
            pltpu.VMEM((N, 2, 128, CH), BF16),
            pltpu.VMEM((256, D), BF16),
            pltpu.VMEM((HB, D), BF16),
            pltpu.VMEM((4, 16, HALF), BF16),
            pltpu.VMEM((32, D), BF16),
            pltpu.VMEM((4, 8, D), F32),
            pltpu.VMEM((3, 8, D), F32),
            pltpu.VMEM((2, 8, D), F32),
            pltpu.VMEM((8, D), F32),
            pltpu.VMEM((16, HALF), BF16),
            pltpu.VMEM((16, HALF), F32),
            pltpu.VMEM((4, 8, HB), F32),
            pltpu.VMEM((5, 128, 128), F32),
            dma((14,)),
            dma((2, N)),
            dma((2, N)),
            dma((2, N)),
            dma((2, N)),
            dma((N,)),
            dma((N,)),
            dma((2, N)),
            dma((2, N)),
            dma((15,)),
            dma((3,)),
            dma((2,)),
            dma(()),
        ],
        compiler_params=pltpu.CompilerParams(
            collective_id=0, has_side_effects=True, vmem_limit_bytes=62 * 2**20
        ),
    )(
        picture_embeds, caption_embeds, img_ids, txt_ids, logit_multiplier, logit_offset,
        branch_entries, rescale_factor.reshape(1, D), entry_projection_matrix, exit_projection_matrix,
    )
    return (image_grad, token_grad)


def solution(mesh):
    in_specs = (
        P(("dp", "tensor"), None),
        P(("dp", "tensor"), None),
        P(),
        P(),
        P(),
        P(),
        P(("dp", "tensor"), None),
        P(),
        P(None, "tensor"),
        P("tensor", None),
    )
    out_specs = (P(("dp", "tensor"), None), P(("dp", "tensor"), None))
    return jax.shard_map(body, mesh=mesh, in_specs=in_specs, out_specs=out_specs, check_vma=False)
```

time: 914 us -> 196 us (0.21)
  waiting for transfers between devices: 753 us -> 0 us
  Pallas kernels: 0 us -> 185 us
  matrix products: 65.7 us -> 0 us
  other arithmetic: 38 us -> 0 us
  blocking collectives: 32.7 us -> 0 us
  between operations: 15.3 us -> 1.99 us
    reduce_scatter x2 -> x0, waiting for transfers between devices: 513 us -> none  [the longest x1 513 us: body(): lax.psum_scatter(trailing_axis_dot(pre_grad, entry_projection_matrix), 't...]
    pallas_call x0 -> x1, Pallas kernels: none -> 185 us  [body(): pl.pallas_call(kernel, out_shape=(jax.ShapeDtypeStruct((8, D), F32), jax....]
    all_gather x2 -> x0, waiting for transfers between devices: 128 us -> none  [the longest x1 125 us: body(): lax.all_gather(branch_entries, 'tensor', axis=0, tiled=True)]
    psum x1 -> x0, waiting for transfers between devices: 109 us -> none  [body(): micro_sums = lax.psum(unit_terms(micro_img), 'tensor')]
    dot_general x4 -> x0, matrix products: 65.7 us -> none  [the longest x2 34.7 us: trailing_axis_dot(): lax.dot_general(left, right, (((1,), (1,)), ((), ())), preferred_element_...]
    all_gather x1 -> x0, blocking collectives: 32.7 us -> none  [body(): lax.all_gather(caption_embeds, 'dp', axis=0, tiled=True)]
    reduce_sum x10 -> x0, other arithmetic: 30.2 us -> none  [the longest x2 12.3 us: layer_stats(): centered = values - jnp.mean(values, axis=-1, keepdims=True)]
  transfers between devices with their start and end apart: 5 -> 0, of which waited for: 4 -> 0; matrix products, arithmetic and copies ran while one was open for 10% -> 0% of each run, Pallas kernels for 0% -> 0%
where the time goes in v1:
time: 196 us
  Pallas kernels  185 us (94%)
  local copies, waits for them, and re-layouts  8.46 us (4%)
  between operations  1.99 us (1%)
    pallas_call x1, Pallas kernels, body(): pl.pallas_call(kernel, out_shape=(jax.ShapeDtypeStruct((8, D), F32), jax....  185 us
    unnamed x2, local copies, waits for them, and re-layouts  5.47 us

profile of v1, /device:TPU:1, one launch (start us, length us, event | category | flops | bytes accessed | tf_op | source)
XLA Modules:
  0.0 195.8 jit_solution(15680002347991445571)
XLA Ops:
  2.0 0.8 reshape.19
  2.8 0.7 reshape.24.img_ids
  3.5 0.8 reshape.21
  4.3 0.7 reshape.22.txt_ids
  5.0 185.3 %shard_map.113 = (f32[8,6144]{1,0:T(8,128)}, f32[128,6144]{1,0:T(8,128)}, bf16[3,6144,768]{2,1,0:T(8,128)(2,1)}) custom-call(bf16[8,6144]{1,0:T(8,128)(2,1)} %pic_ref.1, bf16[8,6144]{1,0:T(8,128)(2,1)} %cap_ref.1, s32[32,1]{1,0:T(8,128)} %reshape.24.img_ids, s32[1,256]{1,0:T(1,128)} %reshape.22.txt_ids, f32[1]{0:T(128)S(6)} %copy.16.mult_ref, ...), custom_call_target="tpu_custom_call" | custom-call | tf_op jit(solution)/shard_map/pallas_call | solution.py:399
  190.3 1.6 copy.18
  191.9 3.9 %copy.19 = f32[128,6144]{1,0:T(8,128)} copy(f32[128,6144]{1,0:T(8,128)} %get-tuple-element.9) | data formatting | bytes 6291456
  (2 shorter events, 0.0 us)

commit v2 on v1

--- a/solution.py
+++ b/solution.py
@@ -15,7 +15,12 @@
 ROWS = 128
 CH = 512
 N = D // CH
-AHEAD = 3
+AHEAD = 4
+LAG_FWD = 2
+LAG_LOAD = 4
+STEP_RELAY, STEP_TEXT, STEP_LOSS, STEP_IMAGE, STEP_COT, STEP_HIDDEN = 2, 5, 6, 8, 9, 11
+AHEAD_FIRST = 2
+STEP_REST = 3
 
 
 def gelu_slope(values):
@@ -29,10 +34,10 @@
 
 
 def kernel(
-    pic_ref, cap_ref, img_ids, txt_ids, mult_ref, offs_ref, tok_ref, gain_ref, w1, wx_hbm,
-    img_out, tok_out, w3,
+    pic_ref, cap_ref, pic_ids, cap_ids, mult_ref, offs_ref, tok_ref, gain_ref, w1, wx_hbm,
+    img_out, scaled_out, stat_out, row_out, w3,
     ln, wbuf, pre, grad, m1o, m2o, m1i, m2i, text, wx, stack, unit, fold, fold_in, tx, exact, cot, cotf, hid, stat,
-    s_send, s_tok, s_fwd, s_z, s_x, s_own, s_for, s_m1, s_m2, s_small, s_hid, s_w, s_wx,
+    s_send, s_tok, s_fwd, s_z, s_x, s_own, s_for, s_m1, s_m2, s_small, s_hid, s_w, s_wx, s_out,
 ):
     d = lax.axis_index("dp")
     t = lax.axis_index("tensor")
@@ -56,20 +61,32 @@
     def wait(ref, sem):
         pltpu.make_async_copy(ref, ref, sem).wait()
 
-    slot = d * 2 + zl
-
-    def text_peer(s):
-        other = (slot + s) % 16
-        return (other // 2, y * 4 + (other % 2) * 2 + c)
+    near = (d, y * 4 + (1 - zl) * 2 + c)
+    near_mate = (d, y * 4 + (1 - zl) * 2 + (1 - c))
+    urgent = jnp.logical_and(zl == 0, c == 0)
+    early = t == 0
 
     bar = pltpu.get_barrier_semaphore()
 
-    def greet(s, _):
-        pl.semaphore_signal(bar, 1, device_id=text_peer(s), device_id_type=MESH)
-        pl.semaphore_signal(bar, 1, device_id=(d, (t + s) % 16), device_id_type=MESH)
-        return 0
-
-    lax.fori_loop(1, 16, greet, 0)
+    def greet(r, _):
+        for peer in (dev((x + r) % 4, y, z, c), dev(x, (y + r) % 4, z, c), dev(x, y, (z + r) % 4, c)):
+            pl.semaphore_signal(bar, 1, device_id=peer, device_id_type=MESH)
+        return 0
+
+    lax.fori_loop(1, 4, greet, 0)
+    for peer in (mate, near_mate):
+        pl.semaphore_signal(bar, 1, device_id=peer, device_id_type=MESH)
+
+    a0, b0 = jnp.where(c == 0, x, z), jnp.where(c == 0, z, x)
+
+    def text_device(a, b):
+        return dev(jnp.where(c == 0, a, b), y, jnp.where(c == 0, b, a), c)
+
+    def text_rows(a, b):
+        x_, z_ = jnp.where(c == 0, a, b), jnp.where(c == 0, b, a)
+        return pl.ds(pl.multiple_of((((z_ // 2) * 4 + x_) * 2 + z_ % 2) * 16, 16), 16)
+
+    text_cols = pl.ds(pl.multiple_of(c * HALF, HALF), HALF)
 
     pltpu.make_async_copy(wx_hbm, wx, s_wx).start()
 
@@ -97,7 +114,7 @@
 
     lax.fori_loop(0, ROWS // 16, norm_rows, 0)
 
-    pl.semaphore_wait(bar, 30)
+    pl.semaphore_wait(bar, 11)
 
     send(tx.at[c], tx.at[c], s_small.at[0], s_small.at[1], mate)
 
@@ -115,15 +132,22 @@
     def chunk(k):
         return pl.ds(pl.multiple_of(k * CH, CH), CH)
 
-    def send_own(k):
+    def send_tokens(k):
         send(ln.at[k, pl.ds(0, 128)], ln.at[k, pl.ds(384, 128)], s_send.at[0], s_tok.at[0, k], yp)
         send(ln.at[k, pl.ds(0, 128)], ln.at[k, pl.ds(128, 128)], s_send.at[1], s_tok.at[1, k], ym)
+
+    def send_weights(k):
         send(w1.at[piece(k, xpar, 0)], w3.at[1, piece(k, xpar, 0)], s_send.at[2], s_z.at[0, k], zm)
         send(w1.at[piece(k, xpar, 1)], w3.at[1, piece(k, xpar, 1)], s_send.at[3], s_z.at[1, k], zp)
         send(w1.at[chunk(k)], w3.at[0, chunk(k)], s_send.at[4], s_own.at[k], mate)
 
     def first(k, _):
-        send_own(k)
+        send_tokens(k)
+
+        @pl.when(k < AHEAD_FIRST)
+        def _():
+            send_weights(k)
+
         return 0
 
     lax.fori_loop(0, AHEAD, first, 0)
@@ -131,22 +155,61 @@
     wait(tx.at[0], s_small.at[1])
     both = jnp.concatenate([tx[0], tx[1]], axis=0)
     mine = jnp.where(c == 0, both[:, :HALF], both[:, HALF:]).astype(BF16)
-    text_rows = pl.ds(pl.multiple_of(slot * 16, 16), 16)
-    text_cols = pl.ds(pl.multiple_of(c * HALF, HALF), HALF)
-    text[text_rows, text_cols] = mine
-
-    def send_texts(s, _):
-        part = text.at[text_rows, text_cols]
-        send(part, part, s_small.at[4], s_small.at[5], text_peer(s))
-        return 0
-
-    lax.fori_loop(1, 16, send_texts, 0)
+    own_rows = text_rows(a0, b0)
+    text[own_rows, text_cols] = mine
+
+    def send_texts(i, _):
+        part = text.at[own_rows, text_cols]
+        send(part, part, s_small.at[4], s_small.at[5], text_device((a0 + i) % 4, b0))
+        return 0
+
+    lax.fori_loop(1, 4, send_texts, 0)
+
+    def second(k, _):
+        send_weights(k)
+        return 0
+
+    lax.fori_loop(AHEAD_FIRST, AHEAD, second, 0)
     pre[...] = jnp.zeros_like(pre)
 
     def load(k, b):
         pltpu.make_async_copy(w1.at[chunk(k)], wbuf.at[b, :, pl.ds(0, HB)], s_w.at[b]).start()
         for j in range(3):
             pltpu.make_async_copy(w3.at[j, chunk(k)], wbuf.at[b, :, pl.ds((j + 1) * HB, HB)], s_w.at[b]).start()
+
+    def ids_of_images():
+        row = pltpu.roll(pic_ids[pl.ds(d, 1), :], (128 - (t % 4) * 8) % 128, 1)
+        image = lax.broadcasted_iota(jnp.int32, (32, 128), 0)
+        lane = lax.broadcasted_iota(jnp.int32, (32, 128), 1)
+        pick = lane == (image // 8) * 32 + image % 8
+        values = jnp.broadcast_to(row.astype(F32), (32, 128))
+        return jnp.sum(jnp.where(pick, values, 0.0), axis=-1, keepdims=True)
+
+    def ids_of_texts():
+        lane = lax.broadcasted_iota(jnp.int32, (1, 128), 1)
+        halves = []
+        for h in range(2):
+            out = jnp.zeros((1, 128), F32)
+            for i in range(4):
+                row = cap_ids[h * 4 + i:h * 4 + i + 1, :]
+                row = pltpu.roll(row, (i * 32 + 128 - y * 32) % 128, 1).astype(F32)
+                out = jnp.where(lane // 32 == i, row, out)
+            halves.append(out)
+        return jnp.concatenate(halves, axis=1)
+
+    def send_sums(r, _):
+        other = (y + r) % 4
+        send(fold.at[other], fold_in.at[r - 1], s_small.at[8], s_small.at[9], dev(x, other, z, c))
+        return 0
+
+    def image_gradient():
+        wait(fold_in, s_small.at[9])
+        total = fold[y] + fold_in[0] + fold_in[1] + fold_in[2]
+        ex = exact[...]
+        scale = stat[2, 0:8, 0:1]
+        g = scale * (total - ex * jnp.sum(ex * total, axis=-1, keepdims=True))
+        img_out[...] = g
+        return g
 
     def gather_step(k, _):
         @pl.when(k < N)
@@ -162,27 +225,28 @@
 
         @pl.when(k + AHEAD < N)
         def _():
-            send_own(k + AHEAD)
-
-        @pl.when(jnp.logical_and(k >= 1, k < N + 1))
-        def _():
-            q = k - 1
+            send_tokens(k + AHEAD)
+            send_weights(k + AHEAD)
+
+        @pl.when(jnp.logical_and(k >= LAG_FWD, k < N + LAG_FWD))
+        def _():
+            q = k - LAG_FWD
             wait(ln.at[0, pl.ds(0, 64)], s_fwd.at[0, q])
             wait(ln.at[0, pl.ds(0, 64)], s_fwd.at[1, q])
             wait(w3.at[1, pl.ds(0, 128)], s_x.at[0, q])
             wait(w3.at[1, pl.ds(0, 128)], s_x.at[1, q])
             send(w3.at[1, chunk(q)], w3.at[2, chunk(q)], s_send.at[9], s_for.at[q], mate)
 
-        @pl.when(jnp.logical_and(k >= 2, k < N + 2))
-        def _():
-            q = k - 2
+        @pl.when(jnp.logical_and(k >= LAG_LOAD, k < N + LAG_LOAD))
+        def _():
+            q = k - LAG_LOAD
             wait(w3.at[0, pl.ds(0, CH)], s_own.at[q])
             wait(w3.at[2, pl.ds(0, CH)], s_for.at[q])
             load(q, q % 2)
 
-        @pl.when(k >= 3)
-        def _():
-            q = k - 3
+        @pl.when(k >= LAG_LOAD + 1)
+        def _():
+            q = k - LAG_LOAD - 1
             b = q % 2
             wait(wbuf.at[b], s_w.at[b])
 
@@ -193,13 +257,24 @@
 
             lax.fori_loop(0, 4, columns, 0)
 
-        @pl.when(k == 1)
-        def _():
-            wait(text.at[pl.ds(0, 240), pl.ds(0, HALF)], s_small.at[5])
+        @pl.when(k == STEP_RELAY)
+        def _():
+            wait(text.at[pl.ds(0, 48), pl.ds(0, HALF)], s_small.at[5])
+
+            def relay(i, _):
+                part = text.at[text_rows((a0 + i // 3) % 4, b0), text_cols]
+                send(part, part, s_small.at[15], s_small.at[16], text_device(a0, (b0 + 1 + i % 3) % 4))
+                return 0
+
+            lax.fori_loop(0, 12, relay, 0)
+
+        @pl.when(k == STEP_TEXT)
+        def _():
+            wait(text.at[pl.ds(0, 192), pl.ds(0, HALF)], s_small.at[16])
             half = text.at[:, text_cols]
             send(half, half, s_small.at[6], s_small.at[7], mate)
 
-        @pl.when(k == 2)
+        @pl.when(k == STEP_LOSS)
         def _():
             wait(stack.at[pl.ds(0, 3)], s_small.at[3])
             wait(text.at[:, pl.ds(0, HALF)], s_small.at[7])
@@ -210,7 +285,7 @@
                 unit[pair * 16:(pair + 1) * 16, HALF:] = jnp.concatenate([a[8:], b[8:]], axis=0).astype(BF16)
             multiplier = mult_ref[0]
             logits = multiplier * dot_nt(unit[...], text[...]) + offs_ref[0]
-            labels = jnp.where(img_ids[...] == txt_ids[...], 1.0, -1.0).astype(F32)
+            labels = jnp.where(ids_of_images() == ids_of_texts(), 1.0, -1.0).astype(F32)
             coef = (-labels * multiplier * jax.nn.sigmoid(-labels * logits)).astype(BF16)
 
             def fold_cols(j, _):
@@ -222,35 +297,33 @@
 
             lax.fori_loop(0, 6, fold_cols, 0)
 
-            def send_sums(r, _):
-                other = (y + r) % 4
-                send(fold.at[other], fold_in.at[r - 1], s_small.at[8], s_small.at[9], dev(x, other, z, c))
+            @pl.when(jnp.logical_and(urgent, y != 0))
+            def _():
+                send_sums(4 - y, 0)
+
+        @pl.when(jnp.logical_and(k == STEP_IMAGE, early))
+        def _():
+            g = image_gradient()
+            cot[...] = jnp.concatenate([g[:, :HALF], g[:, HALF:]], axis=0).astype(BF16)
+
+            def send_cot(r, _):
+                send(cot, cot, s_small.at[10], s_small.at[11], dev(x, (y + r) % 4, z, c))
                 return 0
 
-            lax.fori_loop(1, 4, send_sums, 0)
-
-        @pl.when(k == 4)
-        def _():
-            wait(fold_in, s_small.at[9])
-            total = fold[y] + fold_in[0] + fold_in[1] + fold_in[2]
-            ex = exact[...]
-            scale = stat[2, 0:8, 0:1]
-            g = scale * (total - ex * jnp.sum(ex * total, axis=-1, keepdims=True))
-            img_out[...] = g
-
-            @pl.when(t == 0)
+            lax.fori_loop(1, 4, send_cot, 0)
+
+        @pl.when(jnp.logical_and(k == STEP_COT, urgent))
+        def _():
+            @pl.when(y != 0)
             def _():
-                cot[...] = jnp.concatenate([g[:, :HALF], g[:, HALF:]], axis=0).astype(BF16)
-
-                def send_cot(s, _):
-                    send(cot, cot, s_small.at[10], s_small.at[11], (d, s))
-                    return 0
-
-                lax.fori_loop(1, 16, send_cot, 0)
-
-        @pl.when(k == 6)
-        def _():
-            @pl.when(t != 0)
+                wait(cot, s_small.at[11])
+
+            for peer in (near, near_mate, mate):
+                send(cot, cot, s_small.at[17], s_small.at[11], peer)
+
+        @pl.when(k == STEP_HIDDEN)
+        def _():
+            @pl.when(jnp.logical_not(urgent))
             def _():
                 wait(cot, s_small.at[11])
 
@@ -261,13 +334,22 @@
                 high = dot_nt(cot[...], wx[j * 256:(j + 1) * 256, HALF:])
                 hid[0, :, j * 256:(j + 1) * 256] = low[:8] + high[8:]
             send(hid.at[0], hid.at[1], s_small.at[12], s_hid.at[0], mate)
-            send(hid.at[0], hid.at[2], s_small.at[13], s_hid.at[1], (d, y * 4 + (1 - zl) * 2 + c))
-            send(hid.at[0], hid.at[3], s_small.at[14], s_hid.at[2], (d, y * 4 + (1 - zl) * 2 + (1 - c)))
-
-        return 0
-
-    lax.fori_loop(0, N + 3, gather_step, 0)
+            send(hid.at[0], hid.at[2], s_small.at[13], s_hid.at[1], near)
+            send(hid.at[0], hid.at[3], s_small.at[14], s_hid.at[2], near_mate)
+
+        return 0
+
+    lax.fori_loop(0, N + LAG_LOAD + 1, gather_step, 0)
     load(0, 0)
+
+    def send_rest(r, _):
+        @pl.when(jnp.logical_not(jnp.logical_and(urgent, (y + r) % 4 == 0)))
+        def _():
+            send_sums(r, 0)
+
+        return 0
+
+    lax.fori_loop(1, 4, send_rest, 0)
     for j in range(3):
         wait(hid.at[0], s_hid.at[j])
 
@@ -334,8 +416,13 @@
             e = total * gain_ref[:, cols]
             normed = (tok_ref[:, cols].astype(F32) - stat[0, :, 0:1]) * stat[1, :, 0:1]
             pre[kept(q)] = e
+            pltpu.make_async_copy(pre.at[kept(q)], scaled_out.at[:, cols], s_out).start()
             stat[3] += jnp.broadcast_to(jnp.sum(e, axis=-1, keepdims=True), (128, 128))
             stat[4] += jnp.broadcast_to(jnp.sum(e * normed, axis=-1, keepdims=True), (128, 128))
+
+        @pl.when(jnp.logical_and(n == STEP_REST, jnp.logical_not(early)))
+        def _():
+            image_gradient()
 
         return carry
 
@@ -344,30 +431,29 @@
     lax.fori_loop(0, N + 5, scatter_step, 0)
 
     own_image = t // 2
-
-    def finish(q, _):
-        cols = chunk(q)
-        inverse = stat[1, :, 0:1]
-        normed = (tok_ref[:, cols].astype(F32) - stat[0, :, 0:1]) * inverse
-        cot_cols = pl.ds(pl.multiple_of((q % 6) * CH, CH), CH)
-        row = cotf[pl.ds((q // 6) * 8 + own_image, 1), cot_cols]
-        tok_out[:, cols] = row + inverse * (
-            pre[kept(q)] - stat[3, :, 0:1] * (1.0 / D) - normed * (stat[4, :, 0:1] * (1.0 / D))
-        )
-        return 0
-
-    lax.fori_loop(0, N, finish, 0)
+    for h in range(2):
+        row_out[:, h * HALF:(h + 1) * HALF] = cotf[pl.ds(h * 8 + own_image, 1), :]
+    lane = lax.broadcasted_iota(jnp.int32, (128, 128), 1)
+    means = jnp.where(lane == 2, stat[3], stat[4]) * (1.0 / D)
+    stat_out[...] = jnp.where(lane == 0, stat[0], jnp.where(lane == 1, stat[1], means))
+    wait(scaled_out, s_out)
 
     wait(tx.at[0], s_small.at[0])
     wait(stack.at[pl.ds(0, 3)], s_small.at[2])
-    wait(text.at[pl.ds(0, 240), pl.ds(0, HALF)], s_small.at[4])
+    wait(text.at[pl.ds(0, 48), pl.ds(0, HALF)], s_small.at[4])
+    wait(text.at[pl.ds(0, 192), pl.ds(0, HALF)], s_small.at[15])
     wait(text.at[:, pl.ds(0, HALF)], s_small.at[6])
     wait(fold_in, s_small.at[8])
 
-    @pl.when(t == 0)
+    @pl.when(early)
     def _():
-        for _i in range(15):
+        for _i in range(3):
             wait(cot, s_small.at[10])
+
+    @pl.when(urgent)
+    def _():
+        for _i in range(3):
+            wait(cot, s_small.at[17])
 
     for j in range(3):
         wait(hid.at[0], s_small.at[12 + j])
@@ -386,25 +472,21 @@
     picture_embeds, caption_embeds, picture_match_ids, caption_match_ids, logit_multiplier, logit_offset,
     branch_entries, rescale_factor, entry_projection_matrix, exit_projection_matrix,
 ):
-    d = lax.axis_index("dp")
-    t = lax.axis_index("tensor")
-    img_ids = picture_match_ids.reshape(8, 4, 4, 8)
-    img_ids = lax.dynamic_slice(img_ids, (d, 0, t % 4, 0), (1, 4, 1, 8)).reshape(32, 1)
-    txt_ids = caption_match_ids.reshape(8, 4, 4, 8)
-    txt_ids = lax.dynamic_slice(txt_ids, (0, t // 4, 0, 0), (8, 1, 4, 8)).reshape(1, 256)
     vmem = pl.BlockSpec(memory_space=pltpu.VMEM)
     smem = pl.BlockSpec(memory_space=pltpu.SMEM)
     anyw = pl.BlockSpec(memory_space=pl.ANY)
     dma = pltpu.SemaphoreType.DMA
-    image_grad, token_grad, _ = pl.pallas_call(
+    image_grad, scaled, stats, cot_row, _ = pl.pallas_call(
         kernel,
         out_shape=(
             jax.ShapeDtypeStruct((8, D), F32),
             jax.ShapeDtypeStruct((ROWS, D), F32),
+            jax.ShapeDtypeStruct((ROWS, 128), F32),
+            jax.ShapeDtypeStruct((1, D), F32),
             jax.ShapeDtypeStruct((3, D, HB), BF16),
         ),
         in_specs=[vmem, vmem, vmem, vmem, smem, smem, vmem, vmem, anyw, anyw],
-        out_specs=(vmem, vmem, anyw),
+        out_specs=(vmem, anyw, vmem, vmem, anyw),
         scratch_shapes=[
             pltpu.VMEM((N, 4 * ROWS, CH), BF16),
             pltpu.VMEM((2, CH, 4 * HB), BF16),
@@ -435,18 +517,22 @@
             dma((N,)),
             dma((2, N)),
             dma((2, N)),
-            dma((15,)),
+            dma((18,)),
             dma((3,)),
             dma((2,)),
+            dma(()),
             dma(()),
         ],
         compiler_params=pltpu.CompilerParams(
             collective_id=0, has_side_effects=True, vmem_limit_bytes=62 * 2**20
         ),
     )(
-        picture_embeds, caption_embeds, img_ids, txt_ids, logit_multiplier, logit_offset,
-        branch_entries, rescale_factor.reshape(1, D), entry_projection_matrix, exit_projection_matrix,
+        picture_embeds, caption_embeds, picture_match_ids.reshape(8, 128), caption_match_ids.reshape(8, 128),
+        logit_multiplier, logit_offset, branch_entries, rescale_factor.reshape(1, D), entry_projection_matrix, exit_projection_matrix,
     )
+    inverse = stats[:, 1:2]
+    normed = (branch_entries.astype(F32) - stats[:, 0:1]) * inverse
+    token_grad = cot_row + inverse * (scaled - stats[:, 2:3] - normed * stats[:, 3:4])
     return (image_grad, token_grad)
 
 

time: 196 us -> 170 us (0.87)
  Pallas kernels: 185 us -> 160 us
  local copies, waits for them, and re-layouts: 8.46 us -> 1.9 us
  other arithmetic: 0 us -> 4.63 us
    pallas_call x1, Pallas kernels: 185 us -> 160 us  [body(): pl.pallas_call(kernel, out_shape=(jax.ShapeDtypeStruct((8, D), F32), jax....]
    unnamed x2 -> x5, local copies, waits for them, and re-layouts: 5.47 us -> 0.69 us
    add x0 -> x1, other arithmetic: none -> 4.63 us  [body(): cot_row + inverse * (scaled - stats[:, 2:3] - normed * stats[:, 3:4])]
    reshape x4 -> x0, local copies, waits for them, and re-layouts: 2.95 us -> none  [the longest x1 0.8 us: body(): img_ids = picture_match_ids.reshape(8, 4, 4, 8)]
where the time goes in v2:
time: 170 us; the launch traced here: 169 us
  Pallas kernels  160 us (94%)
  other arithmetic  4.63 us (3%)
  between operations  1.96 us (1%)
  local copies, waits for them, and re-layouts  1.9 us (1%)
    pallas_call x1, Pallas kernels, body(): pl.pallas_call(kernel, out_shape=(jax.ShapeDtypeStruct((8, D), F32), jax....  160 us
    add x1, other arithmetic, body(): cot_row + inverse * (scaled - stats[:, 2:3] - normed * stats[:, 3:4])  4.63 us

profile of v2, /device:TPU:1, one launch (start us, length us, event | category | flops | bytes accessed | tf_op | source)
XLA Modules:
  0.0 168.7 jit_solution(14098056862453801429)
XLA Ops:
  1.9 0.0 copy-start
  1.9 160.2 %shard_map.113 = (f32[8,6144]{1,0:T(8,128)}, f32[128,6144]{1,0:T(8,128)}, f32[128,128]{1,0:T(8,128)}, f32[1,6144]{1,0:T(1,128)}, bf16[3,6144,768]{2,1,0:T(8,128)(2,1)}) custom-call(bf16[8,6144]{1,0:T(8,128)(2,1)} %pic_ref.1, bf16[8,6144]{1,0:T(8,128)(2,1)} %cap_ref.1, s32[8,128]{1,0:T(8,128)} %bitcast.6, s32[8,128]{1,0:T(8,128)} %bitcast.7, ...), custom_call_target="tpu_custom_call" | custom-call | tf_op jit(solution)/shard_map/pallas_call | solution.py:479
  162.1 1.2 slice_reduce_fusion.3
  163.3 0.0 copy-done
  163.3 0.0 copy-start.1
  163.4 4.6 %multiply_add_fusion = f32[128,6144]{1,0:T(8,128)} fusion(bf16[128,6144]{1,0:T(8,128)(2,1)S(1)} %copy-done, f32[128,6144]{1,0:T(8,128)} %get-tuple-element.9, f32[128]{0:T(128)S(1)} %get-tuple-element.11, f32[128]{0:T(128)S(1)} %get-tuple-element.12, f32[128]{0:T(128)S(1)} %get-tuple-element.13, f32[128]{0:T(128)S(1)} %get-tuple-element.10, f32[6144]{0:T(1024)} %bitcast.4), kind=kLoop, calls=%fused_computation | loop fusion | flops 6291456 | bytes 7890944 | tf_op jit(solution)/shard_map/add | solution.py:535
  168.0 0.0 copy-done.1
  168.0 0.7 copy.15
Async XLA Ops:
  1.9 161.4 %copy-start = (bf16[128,6144]{1,0:T(8,128)(2,1)S(1)}, bf16[128,6144]{1,0:T(8,128)(2,1)}, u32[]{:S(2)}) copy-start(bf16[128,6144]{1,0:T(8,128)(2,1)} %tok_ref.1) | copy-start | bytes 4718596
  163.3 4.6 %copy-start.1 = (f32[8,6144]{1,0:T(8,128)S(1)}, f32[8,6144]{1,0:T(8,128)}, u32[]{:S(2)}) copy-start(f32[8,6144]{1,0:T(8,128)} %get-tuple-element.16) | copy-start | bytes 589828

commit v3 on v2

--- a/solution.py
+++ b/solution.py
@@ -15,11 +15,13 @@
 ROWS = 128
 CH = 512
 N = D // CH
-AHEAD = 4
-LAG_FWD = 2
-LAG_LOAD = 4
-STEP_RELAY, STEP_TEXT, STEP_LOSS, STEP_IMAGE, STEP_COT, STEP_HIDDEN = 2, 5, 6, 8, 9, 11
-AHEAD_FIRST = 2
+GC = 256
+G = D // GC
+AHEAD = 6
+LAG_FWD = 3
+LAG_LOAD = 5
+STEP_RELAY, STEP_TEXT, STEP_LOSS, STEP_IMAGE, STEP_COT, STEP_HIDDEN = 4, 10, 12, 16, 18, 21
+AHEAD_FIRST = 4
 STEP_REST = 3
 
 
@@ -108,8 +110,8 @@
         stat[0, rows] = jnp.broadcast_to(mean, (16, 128))
         stat[1, rows] = jnp.broadcast_to(inverse, (16, 128))
         out = (centered * inverse * gain_ref[...]).astype(BF16)
-        for k in range(N):
-            ln[k, rows, :] = out[:, k * CH:(k + 1) * CH]
+        for k in range(G):
+            ln[k, rows, :] = out[:, k * GC:(k + 1) * GC]
         return 0
 
     lax.fori_loop(0, ROWS // 16, norm_rows, 0)
@@ -118,19 +120,16 @@
 
     send(tx.at[c], tx.at[c], s_small.at[0], s_small.at[1], mate)
 
-    def send_images(r, _):
-        send(stack.at[y], stack.at[y], s_small.at[2], s_small.at[3], dev(x, (y + r) % 4, z, c))
-        return 0
-
-    lax.fori_loop(1, 4, send_images, 0)
-
     xpar = x % 2
 
     def piece(k, par, p):
-        return pl.ds(pl.multiple_of(k * CH + par * 256 + p * 128, 128), 128)
+        return pl.ds(pl.multiple_of(k * GC + par * (GC // 2) + p * (GC // 4), GC // 4), GC // 4)
 
     def chunk(k):
         return pl.ds(pl.multiple_of(k * CH, CH), CH)
+
+    def part_of(k):
+        return pl.ds(pl.multiple_of(k * GC, GC), GC)
 
     def send_tokens(k):
         send(ln.at[k, pl.ds(0, 128)], ln.at[k, pl.ds(384, 128)], s_send.at[0], s_tok.at[0, k], yp)
@@ -139,18 +138,25 @@
     def send_weights(k):
         send(w1.at[piece(k, xpar, 0)], w3.at[1, piece(k, xpar, 0)], s_send.at[2], s_z.at[0, k], zm)
         send(w1.at[piece(k, xpar, 1)], w3.at[1, piece(k, xpar, 1)], s_send.at[3], s_z.at[1, k], zp)
-        send(w1.at[chunk(k)], w3.at[0, chunk(k)], s_send.at[4], s_own.at[k], mate)
-
-    def first(k, _):
+        send(w1.at[part_of(k)], w3.at[0, part_of(k)], s_send.at[4], s_own.at[k], mate)
+
+    def first_weights(k, _):
+        send_weights(k)
+        return 0
+
+    lax.fori_loop(0, AHEAD_FIRST, first_weights, 0)
+
+    def first_tokens(k, _):
         send_tokens(k)
-
-        @pl.when(k < AHEAD_FIRST)
-        def _():
-            send_weights(k)
-
-        return 0
-
-    lax.fori_loop(0, AHEAD, first, 0)
+        return 0
+
+    lax.fori_loop(0, AHEAD, first_tokens, 0)
+
+    def send_images(r, _):
+        send(stack.at[y], stack.at[y], s_small.at[2], s_small.at[3], dev(x, (y + r) % 4, z, c))
+        return 0
+
+    lax.fori_loop(1, 4, send_images, 0)
 
     wait(tx.at[0], s_small.at[1])
     both = jnp.concatenate([tx[0], tx[1]], axis=0)
@@ -173,9 +179,13 @@
     pre[...] = jnp.zeros_like(pre)
 
     def load(k, b):
-        pltpu.make_async_copy(w1.at[chunk(k)], wbuf.at[b, :, pl.ds(0, HB)], s_w.at[b]).start()
+        pltpu.make_async_copy(w1.at[part_of(k)], wbuf.at[b, :, pl.ds(0, HB)], s_w.at[b]).start()
         for j in range(3):
-            pltpu.make_async_copy(w3.at[j, chunk(k)], wbuf.at[b, :, pl.ds((j + 1) * HB, HB)], s_w.at[b]).start()
+            pltpu.make_async_copy(w3.at[j, part_of(k)], wbuf.at[b, :, pl.ds((j + 1) * HB, HB)], s_w.at[b]).start()
+
+    def load_chunk(n):
+        for h in range(2):
+            load(2 * n + h, 2 * (n % 2) + h)
 
     def ids_of_images():
         row = pltpu.roll(pic_ids[pl.ds(d, 1), :], (128 - (t % 4) * 8) % 128, 1)
@@ -202,6 +212,13 @@
         send(fold.at[other], fold_in.at[r - 1], s_small.at[8], s_small.at[9], dev(x, other, z, c))
         return 0
 
+    def send_rest(r, _):
+        @pl.when(jnp.logical_not(jnp.logical_and(urgent, (y + r) % 4 == 0)))
+        def _():
+            send_sums(r, 0)
+
+        return 0
+
     def image_gradient():
         wait(fold_in, s_small.at[9])
         total = fold[y] + fold_in[0] + fold_in[1] + fold_in[2]
@@ -212,42 +229,42 @@
         return g
 
     def gather_step(k, _):
-        @pl.when(k < N)
+        @pl.when(k < G)
         def _():
             wait(ln.at[0, pl.ds(0, 128)], s_tok.at[0, k])
             wait(ln.at[0, pl.ds(0, 128)], s_tok.at[1, k])
             send(ln.at[k, pl.ds(384, 64)], ln.at[k, pl.ds(256, 64)], s_send.at[5], s_fwd.at[0, k], yp)
             send(ln.at[k, pl.ds(192, 64)], ln.at[k, pl.ds(320, 64)], s_send.at[6], s_fwd.at[1, k], ym)
-            wait(w3.at[1, pl.ds(0, 128)], s_z.at[0, k])
-            wait(w3.at[1, pl.ds(0, 128)], s_z.at[1, k])
+            wait(w3.at[1, pl.ds(0, GC // 4)], s_z.at[0, k])
+            wait(w3.at[1, pl.ds(0, GC // 4)], s_z.at[1, k])
             send(w3.at[1, piece(k, xpar, 0)], w3.at[1, piece(k, xpar, 0)], s_send.at[7], s_x.at[0, k], xm)
             send(w3.at[1, piece(k, xpar, 1)], w3.at[1, piece(k, xpar, 1)], s_send.at[8], s_x.at[1, k], xp)
 
-        @pl.when(k + AHEAD < N)
+        @pl.when(k + AHEAD < G)
         def _():
             send_tokens(k + AHEAD)
             send_weights(k + AHEAD)
 
-        @pl.when(jnp.logical_and(k >= LAG_FWD, k < N + LAG_FWD))
+        @pl.when(jnp.logical_and(k >= LAG_FWD, k < G + LAG_FWD))
         def _():
             q = k - LAG_FWD
             wait(ln.at[0, pl.ds(0, 64)], s_fwd.at[0, q])
             wait(ln.at[0, pl.ds(0, 64)], s_fwd.at[1, q])
-            wait(w3.at[1, pl.ds(0, 128)], s_x.at[0, q])
-            wait(w3.at[1, pl.ds(0, 128)], s_x.at[1, q])
-            send(w3.at[1, chunk(q)], w3.at[2, chunk(q)], s_send.at[9], s_for.at[q], mate)
-
-        @pl.when(jnp.logical_and(k >= LAG_LOAD, k < N + LAG_LOAD))
+            wait(w3.at[1, pl.ds(0, GC // 4)], s_x.at[0, q])
+            wait(w3.at[1, pl.ds(0, GC // 4)], s_x.at[1, q])
+            send(w3.at[1, part_of(q)], w3.at[2, part_of(q)], s_send.at[9], s_for.at[q], mate)
+
+        @pl.when(jnp.logical_and(k >= LAG_LOAD, k < G + LAG_LOAD))
         def _():
             q = k - LAG_LOAD
-            wait(w3.at[0, pl.ds(0, CH)], s_own.at[q])
-            wait(w3.at[2, pl.ds(0, CH)], s_for.at[q])
-            load(q, q % 2)
+            wait(w3.at[0, pl.ds(0, GC)], s_own.at[q])
+            wait(w3.at[2, pl.ds(0, GC)], s_for.at[q])
+            load(q, q % 4)
 
         @pl.when(k >= LAG_LOAD + 1)
         def _():
             q = k - LAG_LOAD - 1
-            b = q % 2
+            b = q % 4
             wait(wbuf.at[b], s_w.at[b])
 
             def columns(j, _):
@@ -256,6 +273,10 @@
                 return 0
 
             lax.fori_loop(0, 4, columns, 0)
+
+        @pl.when(k == G)
+        def _():
+            lax.fori_loop(1, 4, send_rest, 0)
 
         @pl.when(k == STEP_RELAY)
         def _():
@@ -339,17 +360,9 @@
 
         return 0
 
-    lax.fori_loop(0, N + LAG_LOAD + 1, gather_step, 0)
-    load(0, 0)
-
-    def send_rest(r, _):
-        @pl.when(jnp.logical_not(jnp.logical_and(urgent, (y + r) % 4 == 0)))
-        def _():
-            send_sums(r, 0)
-
-        return 0
-
-    lax.fori_loop(1, 4, send_rest, 0)
+    lax.fori_loop(0, G + LAG_LOAD + 1, gather_step, 0)
+    load_chunk(0)
+
     for j in range(3):
         wait(hid.at[0], s_hid.at[j])
 
@@ -379,13 +392,14 @@
     def scatter_step(n, carry):
         @pl.when(n + 1 < N)
         def _():
-            load(n + 1, (n + 1) % 2)
+            load_chunk(n + 1)
 
         @pl.when(n < N)
         def _():
-            b = n % 2
+            b = 2 * (n % 2)
             wait(wbuf.at[b], s_w.at[b])
-            part = dot_nt(grad[...], wbuf[b])
+            wait(wbuf.at[b + 1], s_w.at[b + 1])
+            part = jnp.concatenate([dot_nt(grad[...], wbuf[b]), dot_nt(grad[...], wbuf[b + 1])], axis=1)
             m1o[n, 0] = part[256:320].astype(BF16)
             m1o[n, 1] = part[320:384].astype(BF16)
             send(m1o.at[n, 0], m1i.at[n, 0], s_send.at[10], s_m1.at[0, n], yp)
@@ -459,13 +473,20 @@
         wait(hid.at[0], s_small.at[12 + j])
     for j in range(2):
         wait(ln.at[:, pl.ds(0, 128)], s_send.at[j])
-        wait(w1.at[pl.ds(0, N * 128)], s_send.at[2 + j])
+        wait(w1.at[pl.ds(0, D // 4)], s_send.at[2 + j])
         wait(ln.at[:, pl.ds(0, 64)], s_send.at[5 + j])
-        wait(w1.at[pl.ds(0, N * 128)], s_send.at[7 + j])
+        wait(w1.at[pl.ds(0, D // 4)], s_send.at[7 + j])
         wait(m1o.at[:, 0], s_send.at[10 + j])
         wait(m2o.at[:, 0], s_send.at[12 + j])
     wait(w1, s_send.at[4])
     wait(w1, s_send.at[9])
+
+
+def finish_kernel(scaled_ref, tok_ref, stat_ref, row_ref, img_ref, img_out, tok_out):
+    inverse = stat_ref[:, 1:2]
+    normed = (tok_ref[...].astype(F32) - stat_ref[:, 0:1]) * inverse
+    tok_out[...] = row_ref[...] + inverse * (scaled_ref[...] - stat_ref[:, 2:3] - normed * stat_ref[:, 3:4])
+    img_out[...] = img_ref[...]
 
 
 def body(
@@ -488,8 +509,8 @@
         in_specs=[vmem, vmem, vmem, vmem, smem, smem, vmem, vmem, anyw, anyw],
         out_specs=(vmem, anyw, vmem, vmem, anyw),
         scratch_shapes=[
-            pltpu.VMEM((N, 4 * ROWS, CH), BF16),
-            pltpu.VMEM((2, CH, 4 * HB), BF16),
+            pltpu.VMEM((G, 4 * ROWS, GC), BF16),
+            pltpu.VMEM((4, GC, 4 * HB), BF16),
             pltpu.VMEM((4 * ROWS, 4 * HB), F32),
             pltpu.VMEM((4 * ROWS, 4 * HB), BF16),
             pltpu.VMEM((N, 2, 64, CH), BF16),
@@ -509,17 +530,17 @@
             pltpu.VMEM((4, 8, HB), F32),
             pltpu.VMEM((5, 128, 128), F32),
             dma((14,)),
-            dma((2, N)),
-            dma((2, N)),
-            dma((2, N)),
-            dma((2, N)),
-            dma((N,)),
-            dma((N,)),
+            dma((2, G)),
+            dma((2, G)),
+            dma((2, G)),
+            dma((2, G)),
+            dma((G,)),
+            dma((G,)),
             dma((2, N)),
             dma((2, N)),
             dma((18,)),
             dma((3,)),
-            dma((2,)),
+            dma((4,)),
             dma(()),
             dma(()),
         ],
@@ -530,10 +551,22 @@
         picture_embeds, caption_embeds, picture_match_ids.reshape(8, 128), caption_match_ids.reshape(8, 128),
         logit_multiplier, logit_offset, branch_entries, rescale_factor.reshape(1, D), entry_projection_matrix, exit_projection_matrix,
     )
-    inverse = stats[:, 1:2]
-    normed = (branch_entries.astype(F32) - stats[:, 0:1]) * inverse
-    token_grad = cot_row + inverse * (scaled - stats[:, 2:3] - normed * stats[:, 3:4])
-    return (image_grad, token_grad)
+    rows = 32
+
+    def block(columns):
+        return pl.BlockSpec((rows, columns), lambda i: (i, 0))
+
+    def whole(count):
+        return pl.BlockSpec((count, D), lambda i: (0, 0))
+
+    return pl.pallas_call(
+        finish_kernel,
+        out_shape=(jax.ShapeDtypeStruct((8, D), F32), jax.ShapeDtypeStruct((ROWS, D), F32)),
+        grid=(ROWS // rows,),
+        in_specs=[block(D), block(D), block(128), whole(1), whole(8)],
+        out_specs=(whole(8), block(D)),
+        compiler_params=pltpu.CompilerParams(vmem_limit_bytes=62 * 2**20),
+    )(scaled, branch_entries, stats, cot_row, image_grad)
 
 
 def solution(mesh):

time: 170 us -> 165 us (0.971)
  other arithmetic: 4.63 us -> 0 us
  Pallas kernels: 160 us -> 163 us
  local copies, waits for them, and re-layouts: 1.9 us -> 0 us
    pallas_call x0 -> x1, Pallas kernels: none -> 5.37 us  [body(): pl.pallas_call(finish_kernel, out_shape=(jax.ShapeDtypeStruct((8, D), F32...]
    add x1 -> x0, other arithmetic: 4.63 us -> none  [body(): cot_row + inverse * (scaled - stats[:, 2:3] - normed * stats[:, 3:4])]
    pallas_call x1, Pallas kernels: 160 us -> 157 us  [body(): pl.pallas_call(kernel, out_shape=(jax.ShapeDtypeStruct((8, D), F32), jax....]
where the time goes in v3:
time: 165 us
  Pallas kernels  163 us (99%)
  between operations  1.93 us (1%)
    pallas_call x1, Pallas kernels, body(): pl.pallas_call(kernel, out_shape=(jax.ShapeDtypeStruct((8, D), F32), jax....  157 us
    pallas_call x1, Pallas kernels, body(): pl.pallas_call(finish_kernel, out_shape=(jax.ShapeDtypeStruct((8, D), F32...  5.37 us

profile of v3, /device:TPU:1, one launch (start us, length us, event | category | flops | bytes accessed | tf_op | source)
XLA Modules:
  0.0 164.5 jit_solution(5091749760847675513)
XLA Ops:
  1.9 157.2 %shard_map.113 = (f32[8,6144]{1,0:T(8,128)}, f32[128,6144]{1,0:T(8,128)}, f32[128,128]{1,0:T(8,128)}, f32[1,6144]{1,0:T(1,128)}, bf16[3,6144,768]{2,1,0:T(8,128)(2,1)}) custom-call(bf16[8,6144]{1,0:T(8,128)(2,1)} %pic_ref.1, bf16[8,6144]{1,0:T(8,128)(2,1)} %cap_ref.1, s32[8,128]{1,0:T(8,128)} %bitcast.4, s32[8,128]{1,0:T(8,128)} %bitcast.5, ...), custom_call_target="tpu_custom_call" | custom-call | tf_op jit(solution)/shard_map/pallas_call | solution.py:500
  159.1 5.4 %shard_map.114 = (f32[8,6144]{1,0:T(8,128)}, f32[128,6144]{1,0:T(8,128)}) custom-call(f32[128,6144]{1,0:T(8,128)} %get-tuple-element.6.scaled_ref, bf16[128,6144]{1,0:T(8,128)(2,1)} %tok_ref.3, f32[128,128]{1,0:T(8,128)} %get-tuple-element.7.stat_ref, f32[1,6144]{1,0:T(1,128)} %get-tuple-element.8.row_ref, f32[8,6144]{1,0:T(8,128)} %get-tuple-element.9.img_ref), custom_call_target="tpu_custom_call" | custom-call | tf_op jit(solution)/shard_map/pallas_call | solution.py:562

commit v4 on v3

--- a/solution.py
+++ b/solution.py
@@ -20,7 +20,7 @@
 AHEAD = 6
 LAG_FWD = 3
 LAG_LOAD = 5
-STEP_RELAY, STEP_TEXT, STEP_LOSS, STEP_IMAGE, STEP_COT, STEP_HIDDEN = 4, 10, 12, 16, 18, 21
+STEP_RELAY, STEP_TEXT, STEP_LOSS, STEP_IMAGE, STEP_COT, STEP_HIDDEN = 4, 10, 12, 17, 20, 24
 AHEAD_FIRST = 4
 STEP_REST = 3
 
@@ -136,8 +136,17 @@
         send(ln.at[k, pl.ds(0, 128)], ln.at[k, pl.ds(128, 128)], s_send.at[1], s_tok.at[1, k], ym)
 
     def send_weights(k):
-        send(w1.at[piece(k, xpar, 0)], w3.at[1, piece(k, xpar, 0)], s_send.at[2], s_z.at[0, k], zm)
-        send(w1.at[piece(k, xpar, 1)], w3.at[1, piece(k, xpar, 1)], s_send.at[3], s_z.at[1, k], zp)
+        @pl.when(k < G - 1)
+        def _():
+            send(w1.at[piece(k, xpar, 0)], w3.at[1, piece(k, xpar, 0)], s_send.at[2], s_z.at[0, k], zm)
+            send(w1.at[piece(k, xpar, 1)], w3.at[1, piece(k, xpar, 1)], s_send.at[3], s_z.at[1, k], zp)
+
+        @pl.when(k == G - 1)
+        def _():
+            low, high = pl.ds(D - GC, GC // 2), pl.ds(D - GC // 2, GC // 2)
+            send(w1.at[low], w3.at[1, low], s_send.at[2], s_z.at[0, k], zm)
+            send(w1.at[high], w3.at[1, high], s_send.at[3], s_z.at[1, k], zp)
+
         send(w1.at[part_of(k)], w3.at[0, part_of(k)], s_send.at[4], s_own.at[k], mate)
 
     def first_weights(k, _):
@@ -235,6 +244,9 @@
             wait(ln.at[0, pl.ds(0, 128)], s_tok.at[1, k])
             send(ln.at[k, pl.ds(384, 64)], ln.at[k, pl.ds(256, 64)], s_send.at[5], s_fwd.at[0, k], yp)
             send(ln.at[k, pl.ds(192, 64)], ln.at[k, pl.ds(320, 64)], s_send.at[6], s_fwd.at[1, k], ym)
+
+        @pl.when(k < G - 1)
+        def _():
             wait(w3.at[1, pl.ds(0, GC // 4)], s_z.at[0, k])
             wait(w3.at[1, pl.ds(0, GC // 4)], s_z.at[1, k])
             send(w3.at[1, piece(k, xpar, 0)], w3.at[1, piece(k, xpar, 0)], s_send.at[7], s_x.at[0, k], xm)
@@ -250,8 +262,17 @@
             q = k - LAG_FWD
             wait(ln.at[0, pl.ds(0, 64)], s_fwd.at[0, q])
             wait(ln.at[0, pl.ds(0, 64)], s_fwd.at[1, q])
-            wait(w3.at[1, pl.ds(0, GC // 4)], s_x.at[0, q])
-            wait(w3.at[1, pl.ds(0, GC // 4)], s_x.at[1, q])
+
+            @pl.when(q < G - 1)
+            def _():
+                wait(w3.at[1, pl.ds(0, GC // 4)], s_x.at[0, q])
+                wait(w3.at[1, pl.ds(0, GC // 4)], s_x.at[1, q])
+
+            @pl.when(q == G - 1)
+            def _():
+                wait(w3.at[1, pl.ds(0, GC // 2)], s_z.at[0, q])
+                wait(w3.at[1, pl.ds(0, GC // 2)], s_z.at[1, q])
+
             send(w3.at[1, part_of(q)], w3.at[2, part_of(q)], s_send.at[9], s_for.at[q], mate)
 
         @pl.when(jnp.logical_and(k >= LAG_LOAD, k < G + LAG_LOAD))
@@ -473,9 +494,9 @@
         wait(hid.at[0], s_small.at[12 + j])
     for j in range(2):
         wait(ln.at[:, pl.ds(0, 128)], s_send.at[j])
-        wait(w1.at[pl.ds(0, D // 4)], s_send.at[2 + j])
+        wait(w1.at[pl.ds(0, D // 4 + GC // 4)], s_send.at[2 + j])
         wait(ln.at[:, pl.ds(0, 64)], s_send.at[5 + j])
-        wait(w1.at[pl.ds(0, D // 4)], s_send.at[7 + j])
+        wait(w1.at[pl.ds(0, D // 4 - GC // 4)], s_send.at[7 + j])
         wait(m1o.at[:, 0], s_send.at[10 + j])
         wait(m2o.at[:, 0], s_send.at[12 + j])
     wait(w1, s_send.at[4])
@@ -551,7 +572,7 @@
         picture_embeds, caption_embeds, picture_match_ids.reshape(8, 128), caption_match_ids.reshape(8, 128),
         logit_multiplier, logit_offset, branch_entries, rescale_factor.reshape(1, D), entry_projection_matrix, exit_projection_matrix,
     )
-    rows = 32
+    rows = 64
 
     def block(columns):
         return pl.BlockSpec((rows, columns), lambda i: (i, 0))

time: 165 us -> 164 us (level)
  Pallas kernels: 163 us -> 160 us
    pallas_call x1, Pallas kernels: 157 us -> 155 us  [body(): pl.pallas_call(kernel, out_shape=(jax.ShapeDtypeStruct((8, D), F32), jax....]
where the time goes in v4:
time: 164 us; the launch traced here: 162 us
  Pallas kernels  160 us (98%)
  between operations  1.93 us (1%)
    pallas_call x1, Pallas kernels, body(): pl.pallas_call(kernel, out_shape=(jax.ShapeDtypeStruct((8, D), F32), jax....  155 us
    pallas_call x1, Pallas kernels, body(): pl.pallas_call(finish_kernel, out_shape=(jax.ShapeDtypeStruct((8, D), F32...  5.02 us

profile of v4, /device:TPU:1, one launch (start us, length us, event | category | flops | bytes accessed | tf_op | source)
XLA Modules:
  0.0 161.9 jit_solution(5707598034490349087)
XLA Ops:
  1.9 155.0 %shard_map.113 = (f32[8,6144]{1,0:T(8,128)}, f32[128,6144]{1,0:T(8,128)}, f32[128,128]{1,0:T(8,128)}, f32[1,6144]{1,0:T(1,128)}, bf16[3,6144,768]{2,1,0:T(8,128)(2,1)}) custom-call(bf16[8,6144]{1,0:T(8,128)(2,1)} %pic_ref.1, bf16[8,6144]{1,0:T(8,128)(2,1)} %cap_ref.1, s32[8,128]{1,0:T(8,128)} %bitcast.4, s32[8,128]{1,0:T(8,128)} %bitcast.5, ...), custom_call_target="tpu_custom_call" | custom-call | tf_op jit(solution)/shard_map/pallas_call | solution.py:521
  156.9 5.0 %shard_map.114 = (f32[8,6144]{1,0:T(8,128)}, f32[128,6144]{1,0:T(8,128)}) custom-call(f32[128,6144]{1,0:T(8,128)} %get-tuple-element.6.scaled_ref, bf16[128,6144]{1,0:T(8,128)(2,1)} %tok_ref.3, f32[128,128]{1,0:T(8,128)} %get-tuple-element.7.stat_ref, f32[1,6144]{1,0:T(1,128)} %get-tuple-element.8.row_ref, f32[8,6144]{1,0:T(8,128)} %get-tuple-element.9.img_ref), custom_call_target="tpu_custom_call" | custom-call | tf_op jit(solution)/shard_map/pallas_call | solution.py:583
